TPU v7x, 32 devices: a whole 2x2x4 slice. The times are simulated.
32 devices in a mesh: bucket: 4 (over x, core), edge: 8 (over z, y).
Axes of the slice: x: 2, y: 2, z: 4, core: 2. Of those that a mesh axis runs over, the one named last changes fastest.
Arguments:
- left_emb: float32 [8192, 400], P(('bucket', 'edge')), may hold values from -20 to 20
- right_emb: float32 [8192, 400], P(('bucket', 'edge')), may hold values from -20 to 20
- left_state: float32 [8192], P(('bucket', 'edge')), may hold values from 0.1 to 10
- right_state: float32 [8192], P(('bucket', 'edge')), may hold values from 0.1 to 10
- relations: float32 [1024, 400], replicated, may hold values from 0.1 to 1.9
- src_rows: int32 [4, 2, 2048], P('bucket', None, 'edge'), may hold values from 0 to 2047, as said below
- dst_rows: int32 [4, 2, 2048], P('bucket', None, 'edge'), may hold values from 0 to 2047, as said below
- rel_ids: int32 [4, 2, 2048], P('bucket', None, 'edge'), may hold values from 0 to 1023
- neg_rows: int32 [4, 2, 2048], P('bucket', None, 'edge'), may hold values from 0 to 2047, as said below
Outputs:
- left_next: float32 [8192, 400], P(('bucket', 'edge'))
- left_state_next: float32 [8192], P(('bucket', 'edge'))
- right_next: float32 [8192, 400], P(('bucket', 'edge'))
- right_state_next: float32 [8192], P(('bucket', 'edge'))
Inputs may be any that keep to these rules, and one draw needn't show every extreme that they name: `src_rows`: of the 256 sources of one bucket, sub-round and index of edge, at most 36 lie in the rows held by any one index of edge; in each bucket and sub-round one index's rows receive exactly 36 from every index. `dst_rows`: likewise for the 256 destinations of one bucket, sub-round and index of edge. `neg_rows`: likewise for the 256 negatives of one bucket, sub-round and index of edge; a block's negatives may repeat rows and may equal its edges' destinations.
All inputs are finite; a program needn't handle non-finite values.
Results may differ from a plain program's by a relative error of at most 0.0037.
Values may be sent and summed in bfloat16 or wider, within the bound.
A program may use at most 64 MiB of HBM per device.

v0:
```python
import functools

import jax
import jax.numpy as jnp
from jax import lax
from jax.experimental import pallas as pl
from jax.experimental.pallas import tpu as pltpu
from jax.sharding import PartitionSpec as P

SUBS = 2
LANE = 128
PACK = 16

sharp = 40.0
rate = 0.5
tiny = 1e-06
guard = 1e-10

f32 = jnp.float32
bf16 = jnp.bfloat16
MESH = pl.DeviceIdType.MESH


def dot(first, second, dims=((1,), (0,))):
    return lax.dot_general(first, second, (dims, ((), ())), preferred_element_type=f32)


def iota(shape, dim):
    return lax.broadcasted_iota(jnp.int32, shape, dim)


def to_column(row):
    n = row.shape[1]
    same = iota((n, n), 0) == iota((n, n), 1)
    return jnp.sum(jnp.where(same, row, 0.0), axis=1, keepdims=True)


def to_row(column):
    n = column.shape[0]
    same = iota((n, n), 0) == iota((n, n), 1)
    return jnp.sum(jnp.where(same, column, 0.0), axis=0, keepdims=True)


def one_hot(where):
    return jnp.where(where, 1.0, 0.0).astype(bf16)


def kernel(
    n, nb, width, cap, slots,
    left_ref, right_ref, lstate_ref, rstate_ref, rel_hbm, src_ref, dst_ref, kind_ref, neg_ref,
    lout_ref, lsout_ref, rout_ref, rsout_ref,
    lbuf, rbuf, lcol, rcol, table, rel_raw, rel_hi, rel_lo, scale,
    place, place_t, pick, pick_t, prow, lrow, flat, fetched, grads,
    wsend, wrecv, msend, mrecv, ssend, srecv,
    wsem_s, wsem_r, msem_s, msem_r, ssem, rel_sem,
):
    rows = left_ref.shape[0]
    edges = src_ref.shape[1]
    wide = lbuf.shape[1]
    main = wide - LANE
    tail = width - main
    groups = slots // PACK
    chunks = main // LANE
    me = lax.axis_index("edge")
    mb = lax.axis_index("bucket")
    after = lax.rem(mb + 1, nb)
    before = lax.rem(mb + nb - 1, nb)

    def partner(j):
        return lax.rem(me + n // 2 + ((j + 1) // 2) * (2 * (j % 2) - 1) + n, n)

    def each_partner(body):
        def step(j, carry):
            body(partner(j))
            return carry
        lax.fori_loop(0, n - 1, step, 0)

    def each_index(body):
        def step(j, carry):
            body(j)
            return carry
        lax.fori_loop(0, n, step, 0)

    barrier = pltpu.get_barrier_semaphore()

    def greet(p):
        pl.semaphore_signal(barrier, inc=1, device_id=(mb, p), device_id_type=MESH)

    each_partner(greet)
    pl.semaphore_signal(barrier, inc=1, device_id=(after, me), device_id_type=MESH)
    pl.semaphore_signal(barrier, inc=1, device_id=(before, me), device_id_type=MESH)

    rel_copy = pltpu.make_async_copy(rel_hbm, rel_raw, rel_sem)
    rel_copy.start()

    def span(p):
        return pl.ds(pl.multiple_of(p * LANE, LANE), LANE)

    earlier = one_hot(iota((edges, edges), 0) < iota((edges, edges), 1))
    holder = iota((n, edges), 0)
    for s in range(SUBS):
        for t, ids_ref in enumerate((src_ref, dst_ref, neg_ref)):
            ids = ids_ref[s : s + 1, :]
            inside = (ids >= holder * rows) & (ids < holder * rows + rows)
            hits = jnp.where(inside, 1.0, 0.0)
            rank = dot(hits.astype(bf16), earlier)
            at = jnp.sum(
                hits * ((holder * LANE + t * cap).astype(f32) + rank), axis=0, keepdims=True
            )
            owner = jnp.sum(hits * holder.astype(f32), axis=0, keepdims=True)
            prow[s : s + 1, t * edges : (t + 1) * edges] = at
            lrow[s : s + 1, t * edges : (t + 1) * edges] = ids.astype(f32) - owner * rows

    def build_place_t(s):
        row = prow[s : s + 1, :].astype(jnp.int32)

        def body(p):
            place_t[span(p), :] = one_hot(iota((LANE, 3 * edges), 0) + p * LANE == row)

        each_index(body)

    def build_place(s):
        for t in range(3):
            column = to_column(prow[s : s + 1, t * edges : (t + 1) * edges]).astype(jnp.int32)

            def body(p):
                place[t * edges : (t + 1) * edges, span(p)] = one_hot(
                    iota((edges, LANE), 1) + p * LANE == column
                )

            each_index(body)

    def ask(s):
        local = lrow[s : s + 1, :]
        upper = iota((8, 3 * edges), 0)
        lhs = jnp.where(upper == 0, local, jnp.where(upper == 1, 1.0, 0.0)).astype(bf16)
        lane = iota((1, LANE), 1)
        offset = jnp.where(lane < cap, 0.0, float(rows))

        def wanted(p):
            found = dot(lhs, place_t[span(p), :], ((1,), (1,)))
            row = jnp.where(found[1:2] > 0.5, found[0:1] + offset, -1.0)
            return jnp.broadcast_to(row, (8, LANE))

        def body(p):
            wsend[s, p] = wanted(p)
            ask_copy(s, p).start()

        each_partner(body)
        wrecv[s, me] = wanted(me)

    def ask_copy(s, p):
        return pltpu.make_async_remote_copy(
            src_ref=wsend.at[s, p], dst_ref=wrecv.at[s, me],
            send_sem=wsem_s.at[s, p], recv_sem=wsem_r.at[s, me],
            device_id=(mb, p), device_id_type=MESH,
        )

    def ask_wait(s):
        def body(p):
            copy = pltpu.make_async_remote_copy(
                src_ref=wsend.at[s, p], dst_ref=wrecv.at[s, p],
                send_sem=wsem_s.at[s, p], recv_sem=wsem_r.at[s, p],
                device_id=(mb, p), device_id_type=MESH,
            )
            copy.wait()

        each_partner(body)

    def build_pick(s):
        def body(p):
            column = to_column(wrecv[s, p][0:1, :]).astype(jnp.int32)
            pick[span(p), :] = one_hot(iota((LANE, 2 * rows), 1) == column)

        each_index(body)

    def build_pick_t(s):
        def body(p):
            row = wrecv[s, p][0:1, :].astype(jnp.int32)
            pick_t[:, span(p)] = one_hot(iota((2 * rows, LANE), 0) == row)

        each_index(body)

    def pack(block, ref):
        for c in range(chunks):
            ref[c * slots : (c + 1) * slots, :] = block[:slots, c * LANE : (c + 1) * LANE].astype(bf16)
        ends = block[:, main:]
        total = ends[:PACK]
        for g in range(1, groups):
            total = total + pltpu.roll(ends[g * PACK : (g + 1) * PACK], g * tail, 1)
        ref[chunks * slots :, :] = total.astype(bf16)

    def exchange(k, make):
        def body(p):
            pack(make(p), msend.at[k, p])
            pltpu.make_async_remote_copy(
                src_ref=msend.at[k, p], dst_ref=mrecv.at[k, me],
                send_sem=msem_s.at[k, p], recv_sem=msem_r.at[k, me],
                device_id=(mb, p), device_id_type=MESH,
            ).start()

        each_partner(body)
        pack(make(me), mrecv.at[k, me])

    keep = iota((PACK, LANE), 1) < tail

    def collect(k):
        def unpack(p):
            at = pl.multiple_of(p * LANE, LANE)
            for c in range(chunks):
                flat[pl.ds(at, slots), c * LANE : (c + 1) * LANE] = mrecv[
                    k, p, c * slots : (c + 1) * slots, :
                ]
            ends = mrecv[k, p, chunks * slots : chunks * slots + PACK, :].astype(f32)
            for g in range(groups):
                part = ends if g == 0 else pltpu.roll(ends, LANE - g * tail, 1)
                flat[pl.ds(at + g * PACK, PACK), main:] = jnp.where(keep, part, 0.0).astype(bf16)

        unpack(me)

        def body(p):
            pltpu.make_async_remote_copy(
                src_ref=msend.at[k, p], dst_ref=mrecv.at[k, p],
                send_sem=msem_s.at[k, p], recv_sem=msem_r.at[k, p],
                device_id=(mb, p), device_id_type=MESH,
            ).wait()
            unpack(p)

        each_partner(body)

    def product(lhs_ref, first, count):
        depth = n * LANE
        step = min(depth, 1024)
        total = None
        for k in range(0, depth, step):
            part = dot(lhs_ref[first : first + count, k : k + step], flat[k : k + step, :])
            total = part if total is None else total + part
        return total

    build_place_t(0)
    pl.semaphore_wait(barrier, n + 1)
    ask(0)

    for buf, ref in ((lbuf, left_ref), (rbuf, right_ref)):
        buf[:, main:] = jnp.zeros((rows, LANE), f32)
        buf[:, :width] = ref[...]
    lcol[...] = jnp.broadcast_to(to_column(lstate_ref[...]), lcol.shape)
    rcol[...] = jnp.broadcast_to(to_column(rstate_ref[...]), rcol.shape)
    table[:rows, :] = lbuf[...].astype(bf16)
    table[rows:, :] = rbuf[...].astype(bf16)
    flat[...] = jnp.zeros(flat.shape, bf16)
    build_place_t(1)
    ask(1)

    rel_count = rel_raw.shape[0]

    def set_scale(s):
        column = to_column(kind_ref[s : s + 1, :].astype(f32)).astype(jnp.int32)
        chosen = one_hot(iota((edges, rel_count), 1) == column)
        scale[s] = dot(chosen, rel_hi[...]) + dot(chosen, rel_lo[...])

    for s in range(SUBS):
        if s == 0:
            ask_wait(0)
            build_pick(0)

        exchange(2 * s, lambda p: dot(pick[span(p), :], table[...]))

        build_place(s)
        build_place_t(s)
        build_pick_t(s)
        if s == 0:
            rel_copy.wait()
            for hi, lo in ((rel_hi, rel_lo),):
                hi[:, main:] = jnp.zeros((rel_count, LANE), bf16)
                lo[:, main:] = jnp.zeros((rel_count, LANE), bf16)
                raw = rel_raw[...]
                upper = raw.astype(bf16)
                hi[:, :width] = upper
                lo[:, :width] = (raw - upper.astype(f32)).astype(bf16)
            set_scale(0)
            set_scale(1)
            ask_wait(1)
            build_pick(1)

        collect(2 * s)
        for t in range(3):
            fetched[t * edges : (t + 1) * edges, :] = product(place, t * edges, edges)

        factor = scale[s]
        source = fetched[:edges, :] * factor
        goal = fetched[edges : 2 * edges, :]
        others = fetched[2 * edges :, :]
        inv_q = lax.rsqrt(jnp.sum(source * source, axis=1, keepdims=True) + tiny)
        inv_t = lax.rsqrt(jnp.sum(goal * goal, axis=1, keepdims=True) + tiny)
        inv_n = lax.rsqrt(jnp.sum(others * others, axis=1, keepdims=True) + tiny)
        query = source * inv_q
        target = goal * inv_t
        noise = others * inv_n
        query_half = query.astype(bf16)
        noise_half = noise.astype(bf16)
        positive = sharp * jnp.sum(query * target, axis=1, keepdims=True)
        scores = sharp * dot(query_half, noise_half, ((1,), (1,)))
        raised = jnp.exp(positive)
        spread = jnp.exp(scores)
        total = raised + jnp.sum(spread, axis=1, keepdims=True)
        miss = raised / total - 1.0
        weights = (spread / total).astype(bf16)
        query_grad = sharp * (miss * target + dot(weights, noise_half))
        noise_grad = sharp * dot(weights, query_half, ((0,), (0,)))
        along_q = jnp.sum(query * query_grad, axis=1, keepdims=True)
        along_n = jnp.sum(noise * noise_grad, axis=1, keepdims=True)
        grads[:edges, :] = ((query_grad - query * along_q) * inv_q * factor).astype(bf16)
        grads[edges : 2 * edges, :] = (
            (sharp * miss * query - target * (miss * positive)) * inv_t
        ).astype(bf16)
        grads[2 * edges :, :] = ((noise_grad - noise * along_n) * inv_n).astype(bf16)

        exchange(2 * s + 1, lambda p: dot(place_t[span(p), :], grads[...]))
        collect(2 * s + 1)

        for buf, col, first in ((rbuf, rcol, rows), (lbuf, lcol, 0)):
            grad = product(pick_t, first, rows)
            state = col[...][:, 0:1] + jnp.sum(grad * grad, axis=1, keepdims=True) * (1.0 / width)
            col[...] = jnp.broadcast_to(state, col.shape)
            new = buf[...] - rate * grad / (jnp.sqrt(state) + guard)
            buf[...] = new
            if s + 1 < SUBS:
                table[first : first + rows, :] = new.astype(bf16)
            elif first:
                deep = rows * tail // LANE
                for c in range(chunks):
                    ssend[c * rows : (c + 1) * rows, :] = new[:, c * LANE : (c + 1) * LANE]
                ends = new[:, main:]
                packed = ends[:deep]
                for g in range(1, LANE // tail):
                    packed = packed + pltpu.roll(ends[g * deep : (g + 1) * deep], g * tail, 1)
                base = chunks * rows
                ssend[base : base + deep, :] = packed
                base = base + deep
                for c in range(rows // LANE):
                    ssend[base + 8 * c : base + 8 * c + 8, :] = jnp.broadcast_to(
                        to_row(state[c * LANE : (c + 1) * LANE]), (8, LANE)
                    )
                shift = pltpu.make_async_remote_copy(
                    src_ref=ssend, dst_ref=srecv, send_sem=ssem.at[0], recv_sem=ssem.at[1],
                    device_id=(after, me), device_id_type=MESH,
                )
                shift.start()

    lout_ref[...] = lbuf[:, :width]
    lsout_ref[...] = to_row(lcol[...][:, 0:1])
    shift.wait()
    deep = rows * tail // LANE
    rout_ref[:, :main] = jnp.concatenate(
        [srecv[c * rows : (c + 1) * rows, :] for c in range(chunks)], axis=1
    )
    base = chunks * rows
    ends = srecv[base : base + deep, :]
    for g in range(LANE // tail):
        part = ends if g == 0 else pltpu.roll(ends, LANE - g * tail, 1)
        rout_ref[g * deep : (g + 1) * deep, main:] = part[:, :tail]
    base = base + deep
    for c in range(rows // LANE):
        rsout_ref[:, c * LANE : (c + 1) * LANE] = srecv[base + 8 * c : base + 8 * c + 1, :]


def on_device(
    left_emb, right_emb, left_state, right_state, relations, src_rows, dst_rows, rel_ids, neg_rows
):
    rows, width = left_emb.shape
    rel_count = relations.shape[0]
    n = lax.axis_size("edge")
    nb = lax.axis_size("bucket")
    edges = src_rows.shape[2]
    cap = edges // n + 4
    slots = -(-3 * cap // PACK) * PACK
    wide = -(-width // LANE) * LANE
    chunks = wide // LANE - 1
    message = chunks * slots + PACK
    shifted = chunks * rows + rows * (width - chunks * LANE) // LANE + 8 * (rows // LANE)
    vmem = pl.BlockSpec(memory_space=pltpu.VMEM)
    out = pl.pallas_call(
        functools.partial(kernel, n, nb, width, cap, slots),
        out_shape=(
            jax.ShapeDtypeStruct((rows, width), f32),
            jax.ShapeDtypeStruct((1, rows), f32),
            jax.ShapeDtypeStruct((rows, width), f32),
            jax.ShapeDtypeStruct((1, rows), f32),
        ),
        in_specs=[vmem] * 4 + [pl.BlockSpec(memory_space=pl.ANY)] + [vmem] * 4,
        out_specs=(vmem,) * 4,
        scratch_shapes=[
            pltpu.VMEM((rows, wide), f32),
            pltpu.VMEM((rows, wide), f32),
            pltpu.VMEM((rows, LANE), f32),
            pltpu.VMEM((rows, LANE), f32),
            pltpu.VMEM((2 * rows, wide), bf16),
            pltpu.VMEM((rel_count, width), f32),
            pltpu.VMEM((rel_count, wide), bf16),
            pltpu.VMEM((rel_count, wide), bf16),
            pltpu.VMEM((SUBS, edges, wide), f32),
            pltpu.VMEM((3 * edges, n * LANE), bf16),
            pltpu.VMEM((n * LANE, 3 * edges), bf16),
            pltpu.VMEM((n * LANE, 2 * rows), bf16),
            pltpu.VMEM((2 * rows, n * LANE), bf16),
            pltpu.VMEM((8, 3 * edges), f32),
            pltpu.VMEM((8, 3 * edges), f32),
            pltpu.VMEM((n * LANE, wide), bf16),
            pltpu.VMEM((3 * edges, wide), f32),
            pltpu.VMEM((3 * edges, wide), bf16),
            pltpu.VMEM((SUBS, n, 8, LANE), f32),
            pltpu.VMEM((SUBS, n, 8, LANE), f32),
            pltpu.VMEM((2 * SUBS, n, message, LANE), bf16),
            pltpu.VMEM((2 * SUBS, n, message, LANE), bf16),
            pltpu.VMEM((shifted, LANE), f32),
            pltpu.VMEM((shifted, LANE), f32),
            pltpu.SemaphoreType.DMA((SUBS, n)),
            pltpu.SemaphoreType.DMA((SUBS, n)),
            pltpu.SemaphoreType.DMA((2 * SUBS, n)),
            pltpu.SemaphoreType.DMA((2 * SUBS, n)),
            pltpu.SemaphoreType.DMA((2,)),
            pltpu.SemaphoreType.DMA,
        ],
        compiler_params=pltpu.CompilerParams(
            collective_id=0, has_side_effects=True, vmem_limit_bytes=56 * 1024 * 1024
        ),
    )(
        left_emb, right_emb, left_state.reshape(1, rows), right_state.reshape(1, rows),
        relations, src_rows[0], dst_rows[0], rel_ids[0], neg_rows[0],
    )
    return out[0], out[1].reshape(rows), out[2], out[3].reshape(rows)


def solution(mesh):
    return jax.shard_map(
        on_device,
        mesh=mesh,
        in_specs=(
            P(("bucket", "edge"), None),
            P(("bucket", "edge"), None),
            P(("bucket", "edge")),
            P(("bucket", "edge")),
            P(),
            P("bucket", None, "edge"),
            P("bucket", None, "edge"),
            P("bucket", None, "edge"),
            P("bucket", None, "edge"),
        ),
        out_specs=(
            P(("bucket", "edge"), None),
            P(("bucket", "edge")),
            P(("bucket", "edge"), None),
            P(("bucket", "edge")),
        ),
        check_vma=False,
    )
```

profile of v0, /device:TPU:16, one launch (start us, length us, event | category | flops | bytes accessed | tf_op | source)
XLA Modules:
  0.0 98.1 jit_solution(13894851200219307406)
XLA Ops:
  0.6 0.0 copy-start
  0.6 2.1 %copy.13.left_ref = f32[256,400]{1,0:T(8,128)} copy(f32[256,400]{0,1:T(8,128)} %param.9) | data formatting | bytes 819200 | tf_op args[0]
  2.8 2.0 %copy.14.right_ref = f32[256,400]{1,0:T(8,128)} copy(f32[256,400]{0,1:T(8,128)} %param.10) | data formatting | bytes 819200 | tf_op args[1]
  4.8 0.0 copy-done
  4.8 1.8 %copy.15.rel_hbm = f32[1024,400]{1,0:T(8,128)} copy(f32[1024,400]{0,1:T(8,128)S(1)} %copy-done) | data formatting | bytes 3276800 | tf_op args[4]
  6.6 85.1 %shard_map.120 = (f32[256,400]{1,0:T(8,128)}, f32[1,256]{1,0:T(1,128)}, f32[256,400]{1,0:T(8,128)}, f32[1,256]{1,0:T(1,128)}) custom-call(f32[256,400]{1,0:T(8,128)} %copy.13.left_ref, f32[256,400]{1,0:T(8,128)} %copy.14.right_ref, f32[1,256]{1,0:T(1,128)} %bitcast.12, f32[1,256]{1,0:T(1,128)} %bitcast.13, f32[1024,400]{1,0:T(8,128)} %copy.15.rel_hbm, ...), custom_call_target="tpu_custom_call" | custom-call | tf_op jit(solution)/shard_map/pallas_call | solution.py:383
  91.7 2.0 %copy.16 = f32[256,400]{0,1:T(8,128)} copy(f32[256,400]{1,0:T(8,128)} %get-tuple-element.12) | data formatting | bytes 819200
  93.7 2.0 %copy.17 = f32[256,400]{0,1:T(8,128)} copy(f32[256,400]{1,0:T(8,128)} %get-tuple-element.14) | data formatting | bytes 819200
  95.7 1.2 %copy.20 = f32[256]{0:T(256)} copy(f32[256]{0:T(256)} %bitcast.15) | data formatting | bytes 2048
  96.9 1.2 %copy.21 = f32[256]{0:T(256)} copy(f32[256]{0:T(256)} %bitcast.14) | data formatting | bytes 2048
Async XLA Ops:
  0.6 4.1 %copy-start = (f32[1024,400]{0,1:T(8,128)S(1)}, f32[1024,400]{0,1:T(8,128)}, u32[]{:S(2)}) copy-start(f32[1024,400]{0,1:T(8,128)} %param.13) | copy-start | bytes 4915204
where the time goes:
time: 98.5 us; the launch traced here: 98.1 us
  Pallas kernels  85.1 us (86%)
  local copies, waits for them, and re-layouts  12.4 us (13%)
    pallas_call x1, Pallas kernels, on_device(): pl.pallas_call(functools.partial(kernel, n, nb, width, cap, slots), out_s...  85.1 us
    unnamed x9, local copies, waits for them, and re-layouts  12.4 us

commit v1 on v0

--- a/solution.py
+++ b/solution.py
@@ -51,10 +51,10 @@
     lout_ref, lsout_ref, rout_ref, rsout_ref,
     lbuf, rbuf, lcol, rcol, table, rel_raw, rel_hi, rel_lo, scale,
     place, place_t, pick, pick_t, prow, lrow, flat, fetched, grads,
-    wsend, wrecv, msend, mrecv, ssend, srecv,
+    wsend, wrecv, msend, mrecv, base_send, base_recv, step_send, step_recv, hist_send, hist_recv,
     wsem_s, wsem_r, msem_s, msem_r, ssem, rel_sem,
 ):
-    rows = left_ref.shape[0]
+    rows = left_ref.shape[1]
     edges = src_ref.shape[1]
     wide = lbuf.shape[1]
     main = wide - LANE
@@ -92,6 +92,12 @@
 
     rel_copy = pltpu.make_async_copy(rel_hbm, rel_raw, rel_sem)
     rel_copy.start()
+
+    def onward(source, goal, i):
+        return pltpu.make_async_remote_copy(
+            src_ref=source, dst_ref=goal, send_sem=ssem.at[0, i], recv_sem=ssem.at[1, i],
+            device_id=(after, me), device_id_type=MESH,
+        )
 
     def span(p):
         return pl.ds(pl.multiple_of(p * LANE, LANE), LANE)
@@ -242,8 +248,7 @@
     ask(0)
 
     for buf, ref in ((lbuf, left_ref), (rbuf, right_ref)):
-        buf[:, main:] = jnp.zeros((rows, LANE), f32)
-        buf[:, :width] = ref[...]
+        buf[...] = jnp.concatenate([ref[...], jnp.zeros((wide - width, rows), f32)], axis=0).T
     lcol[...] = jnp.broadcast_to(to_column(lstate_ref[...]), lcol.shape)
     rcol[...] = jnp.broadcast_to(to_column(rstate_ref[...]), rcol.shape)
     table[:rows, :] = lbuf[...].astype(bf16)
@@ -252,12 +257,13 @@
     build_place_t(1)
     ask(1)
 
-    rel_count = rel_raw.shape[0]
+    rel_count = rel_raw.shape[1]
 
     def set_scale(s):
         column = to_column(kind_ref[s : s + 1, :].astype(f32)).astype(jnp.int32)
         chosen = one_hot(iota((edges, rel_count), 1) == column)
-        scale[s] = dot(chosen, rel_hi[...]) + dot(chosen, rel_lo[...])
+        last = ((1,), (1,))
+        scale[s] = dot(chosen, rel_hi[...], last) + dot(chosen, rel_lo[...], last)
 
     for s in range(SUBS):
         if s == 0:
@@ -266,18 +272,20 @@
 
         exchange(2 * s, lambda p: dot(pick[span(p), :], table[...]))
 
+        if s == SUBS - 1:
+            base_send[...] = rbuf[...].T[:width, :]
+            onward(base_send, base_recv, 0).start()
         build_place(s)
         build_place_t(s)
         build_pick_t(s)
         if s == 0:
             rel_copy.wait()
-            for hi, lo in ((rel_hi, rel_lo),):
-                hi[:, main:] = jnp.zeros((rel_count, LANE), bf16)
-                lo[:, main:] = jnp.zeros((rel_count, LANE), bf16)
-                raw = rel_raw[...]
-                upper = raw.astype(bf16)
-                hi[:, :width] = upper
-                lo[:, :width] = (raw - upper.astype(f32)).astype(bf16)
+            for ref in (rel_hi, rel_lo):
+                ref[width:, :] = jnp.zeros((wide - width, rel_count), bf16)
+            raw = rel_raw[...]
+            upper = raw.astype(bf16)
+            rel_hi[:width, :] = upper
+            rel_lo[:width, :] = (raw - upper.astype(f32)).astype(bf16)
             set_scale(0)
             set_scale(1)
             ask_wait(1)
@@ -323,46 +331,31 @@
             grad = product(pick_t, first, rows)
             state = col[...][:, 0:1] + jnp.sum(grad * grad, axis=1, keepdims=True) * (1.0 / width)
             col[...] = jnp.broadcast_to(state, col.shape)
-            new = buf[...] - rate * grad / (jnp.sqrt(state) + guard)
-            buf[...] = new
-            if s + 1 < SUBS:
-                table[first : first + rows, :] = new.astype(bf16)
-            elif first:
-                deep = rows * tail // LANE
-                for c in range(chunks):
-                    ssend[c * rows : (c + 1) * rows, :] = new[:, c * LANE : (c + 1) * LANE]
-                ends = new[:, main:]
-                packed = ends[:deep]
-                for g in range(1, LANE // tail):
-                    packed = packed + pltpu.roll(ends[g * deep : (g + 1) * deep], g * tail, 1)
-                base = chunks * rows
-                ssend[base : base + deep, :] = packed
-                base = base + deep
-                for c in range(rows // LANE):
-                    ssend[base + 8 * c : base + 8 * c + 8, :] = jnp.broadcast_to(
-                        to_row(state[c * LANE : (c + 1) * LANE]), (8, LANE)
-                    )
-                shift = pltpu.make_async_remote_copy(
-                    src_ref=ssend, dst_ref=srecv, send_sem=ssem.at[0], recv_sem=ssem.at[1],
-                    device_id=(after, me), device_id_type=MESH,
-                )
-                shift.start()
-
-    lout_ref[...] = lbuf[:, :width]
+            step = rate * grad / (jnp.sqrt(state) + guard)
+            if s + 1 == SUBS and first:
+                step_send[...] = step.T[:width, :].astype(bf16)
+                onward(step_send, step_recv, 1).start()
+                hist_send[...] = jnp.broadcast_to(to_row(state), hist_send.shape)
+                onward(hist_send, hist_recv, 2).start()
+            else:
+                new = buf[...] - step
+                buf[...] = new
+                if s + 1 < SUBS:
+                    table[first : first + rows, :] = new.astype(bf16)
+
+    lout_ref[...] = lbuf[...].T[:width, :]
     lsout_ref[...] = to_row(lcol[...][:, 0:1])
-    shift.wait()
-    deep = rows * tail // LANE
-    rout_ref[:, :main] = jnp.concatenate(
-        [srecv[c * rows : (c + 1) * rows, :] for c in range(chunks)], axis=1
-    )
-    base = chunks * rows
-    ends = srecv[base : base + deep, :]
-    for g in range(LANE // tail):
-        part = ends if g == 0 else pltpu.roll(ends, LANE - g * tail, 1)
-        rout_ref[g * deep : (g + 1) * deep, main:] = part[:, :tail]
-    base = base + deep
-    for c in range(rows // LANE):
-        rsout_ref[:, c * LANE : (c + 1) * LANE] = srecv[base + 8 * c : base + 8 * c + 1, :]
+    for i, (source, goal) in enumerate(
+        ((base_send, base_recv), (step_send, step_recv), (hist_send, hist_recv))
+    ):
+        onward(source, goal, i).wait()
+    rout_ref[...] = base_recv[...] - step_recv[...].astype(f32)
+    rsout_ref[...] = hist_recv[0:1, :]
+
+
+def finish(*refs):
+    for i in range(4):
+        refs[4 + i][...] = refs[i][...]
 
 
 def on_device(
@@ -378,16 +371,14 @@
     wide = -(-width // LANE) * LANE
     chunks = wide // LANE - 1
     message = chunks * slots + PACK
-    shifted = chunks * rows + rows * (width - chunks * LANE) // LANE + 8 * (rows // LANE)
     vmem = pl.BlockSpec(memory_space=pltpu.VMEM)
+    shapes = (
+        jax.ShapeDtypeStruct((width, rows), f32),
+        jax.ShapeDtypeStruct((1, rows), f32),
+    ) * 2
     out = pl.pallas_call(
         functools.partial(kernel, n, nb, width, cap, slots),
-        out_shape=(
-            jax.ShapeDtypeStruct((rows, width), f32),
-            jax.ShapeDtypeStruct((1, rows), f32),
-            jax.ShapeDtypeStruct((rows, width), f32),
-            jax.ShapeDtypeStruct((1, rows), f32),
-        ),
+        out_shape=shapes,
         in_specs=[vmem] * 4 + [pl.BlockSpec(memory_space=pl.ANY)] + [vmem] * 4,
         out_specs=(vmem,) * 4,
         scratch_shapes=[
@@ -396,9 +387,9 @@
             pltpu.VMEM((rows, LANE), f32),
             pltpu.VMEM((rows, LANE), f32),
             pltpu.VMEM((2 * rows, wide), bf16),
-            pltpu.VMEM((rel_count, width), f32),
-            pltpu.VMEM((rel_count, wide), bf16),
-            pltpu.VMEM((rel_count, wide), bf16),
+            pltpu.VMEM((width, rel_count), f32),
+            pltpu.VMEM((wide, rel_count), bf16),
+            pltpu.VMEM((wide, rel_count), bf16),
             pltpu.VMEM((SUBS, edges, wide), f32),
             pltpu.VMEM((3 * edges, n * LANE), bf16),
             pltpu.VMEM((n * LANE, 3 * edges), bf16),
@@ -413,23 +404,30 @@
             pltpu.VMEM((SUBS, n, 8, LANE), f32),
             pltpu.VMEM((2 * SUBS, n, message, LANE), bf16),
             pltpu.VMEM((2 * SUBS, n, message, LANE), bf16),
-            pltpu.VMEM((shifted, LANE), f32),
-            pltpu.VMEM((shifted, LANE), f32),
+            pltpu.VMEM((width, rows), f32),
+            pltpu.VMEM((width, rows), f32),
+            pltpu.VMEM((width, rows), bf16),
+            pltpu.VMEM((width, rows), bf16),
+            pltpu.VMEM((8, rows), f32),
+            pltpu.VMEM((8, rows), f32),
             pltpu.SemaphoreType.DMA((SUBS, n)),
             pltpu.SemaphoreType.DMA((SUBS, n)),
             pltpu.SemaphoreType.DMA((2 * SUBS, n)),
             pltpu.SemaphoreType.DMA((2 * SUBS, n)),
-            pltpu.SemaphoreType.DMA((2,)),
+            pltpu.SemaphoreType.DMA((2, 3)),
             pltpu.SemaphoreType.DMA,
         ],
         compiler_params=pltpu.CompilerParams(
             collective_id=0, has_side_effects=True, vmem_limit_bytes=56 * 1024 * 1024
         ),
     )(
-        left_emb, right_emb, left_state.reshape(1, rows), right_state.reshape(1, rows),
-        relations, src_rows[0], dst_rows[0], rel_ids[0], neg_rows[0],
+        left_emb.T, right_emb.T, left_state.reshape(1, rows), right_state.reshape(1, rows),
+        relations.T, src_rows[0], dst_rows[0], rel_ids[0], neg_rows[0],
     )
-    return out[0], out[1].reshape(rows), out[2], out[3].reshape(rows)
+    out = pl.pallas_call(
+        finish, out_shape=shapes, in_specs=[vmem] * 4, out_specs=(vmem,) * 4
+    )(*out)
+    return out[0].T, out[1].reshape(rows), out[2].T, out[3].reshape(rows)
 
 
 def solution(mesh):

time: 98.5 us -> 86.4 us (0.88); the launches traced: 98.1 us -> 84.9 us
  local copies, waits for them, and re-layouts: 12.4 us -> 0 us
    unnamed x9 -> x0, local copies, waits for them, and re-layouts: 12.4 us -> none
    pallas_call x1, Pallas kernels: 85.1 us -> 82.2 us  [on_device(): pl.pallas_call(functools.partial(kernel, n, nb, width, cap, slots), out_s...]
    pallas_call x0 -> x1, Pallas kernels: none -> 2.05 us  [on_device(): pl.pallas_call(finish, out_shape=shapes, in_specs=[vmem] * 4, out_specs=(...]
where the time goes in v1:
time: 86.4 us; the launch traced here: 84.9 us
  Pallas kernels  84.3 us (98%)
    pallas_call x1, Pallas kernels, on_device(): pl.pallas_call(functools.partial(kernel, n, nb, width, cap, slots), out_s...  82.2 us
    pallas_call x1, Pallas kernels, on_device(): pl.pallas_call(finish, out_shape=shapes, in_specs=[vmem] * 4, out_specs=(...  2.05 us

profile of v1, /device:TPU:16, one launch (start us, length us, event | category | flops | bytes accessed | tf_op | source)
XLA Modules:
  0.0 84.9 jit_solution(12320544788848202026)
XLA Ops:
  0.6 82.2 %shard_map.120 = (f32[400,256]{1,0:T(8,128)}, f32[1,256]{1,0:T(1,128)}, f32[400,256]{1,0:T(8,128)}, f32[1,256]{1,0:T(1,128)}) custom-call(f32[400,256]{1,0:T(8,128)} %bitcast.14, f32[400,256]{1,0:T(8,128)} %bitcast.15, f32[1,256]{1,0:T(1,128)} %bitcast.20, f32[1,256]{1,0:T(1,128)} %bitcast.21, f32[400,1024]{1,0:T(8,128)} %bitcast.13, s32[2,256]{1,0:T(2,128)} %bitcast.16, ...), custom_call_target="tpu_custom_call" | custom-call | tf_op jit(solution)/shard_map/pallas_call | solution.py:379
  82.9 2.1 %shard_map.121 = (f32[400,256]{1,0:T(8,128)}, f32[1,256]{1,0:T(1,128)}, f32[400,256]{1,0:T(8,128)}, f32[1,256]{1,0:T(1,128)}) custom-call(f32[400,256]{1,0:T(8,128)} %get-tuple-element.12.refs_0_, f32[1,256]{1,0:T(1,128)} %get-tuple-element.13.refs_1_, f32[400,256]{1,0:T(8,128)} %get-tuple-element.14.refs_2_, f32[1,256]{1,0:T(1,128)} %get-tuple-element.15.refs_3_), custom_call_target="tpu_custom_call" | custom-call | tf_op jit(solution)/shard_map/pallas_call | solution.py:427

commit v2 on v1

--- a/solution.py
+++ b/solution.py
@@ -66,14 +66,31 @@
     after = lax.rem(mb + 1, nb)
     before = lax.rem(mb + nb - 1, nb)
 
-    def partner(j):
-        return lax.rem(me + n // 2 + ((j + 1) // 2) * (2 * (j % 2) - 1) + n, n)
+    half = n // 2
+    mine = (me // half) * half
+    other = half - mine
+
+    def far(j):
+        return other + lax.rem(me + j, half)
+
+    def near(j):
+        return mine + lax.rem(me + j, half)
+
+    def each_far(body):
+        def step(j, carry):
+            body(far(j))
+            return carry
+        lax.fori_loop(0, half, step, 0)
+
+    def each_near(body):
+        def step(j, carry):
+            body(near(j))
+            return carry
+        lax.fori_loop(1, half, step, 0)
 
     def each_partner(body):
-        def step(j, carry):
-            body(partner(j))
-            return carry
-        lax.fori_loop(0, n - 1, step, 0)
+        each_far(body)
+        each_near(body)
 
     def each_index(body):
         def step(j, carry):
@@ -143,17 +160,14 @@
         lane = iota((1, LANE), 1)
         offset = jnp.where(lane < cap, 0.0, float(rows))
 
-        def wanted(p):
-            found = dot(lhs, place_t[span(p), :], ((1,), (1,)))
-            row = jnp.where(found[1:2] > 0.5, found[0:1] + offset, -1.0)
-            return jnp.broadcast_to(row, (8, LANE))
-
-        def body(p):
-            wsend[s, p] = wanted(p)
-            ask_copy(s, p).start()
-
-        each_partner(body)
-        wrecv[s, me] = wanted(me)
+        found = dot(lhs, place_t[...], ((1,), (1,)))
+        for p in range(n):
+            part = found[:, p * LANE : (p + 1) * LANE]
+            row = jnp.where(part[1:2] > 0.5, part[0:1] + offset, -1.0)
+            wsend[s, p] = jnp.broadcast_to(row, (8, LANE))
+
+        each_partner(lambda p: ask_copy(s, p).start())
+        wrecv[s, me] = wsend[s, me]
 
     def ask_copy(s, p):
         return pltpu.make_async_remote_copy(
@@ -187,61 +201,135 @@
 
         each_index(body)
 
-    def pack(block, ref):
-        for c in range(chunks):
-            ref[c * slots : (c + 1) * slots, :] = block[:slots, c * LANE : (c + 1) * LANE].astype(bf16)
-        ends = block[:, main:]
-        total = ends[:PACK]
-        for g in range(1, groups):
-            total = total + pltpu.roll(ends[g * PACK : (g + 1) * PACK], g * tail, 1)
-        ref[chunks * slots :, :] = total.astype(bf16)
-
-    def exchange(k, make):
-        def body(p):
-            pack(make(p), msend.at[k, p])
-            pltpu.make_async_remote_copy(
-                src_ref=msend.at[k, p], dst_ref=mrecv.at[k, me],
-                send_sem=msem_s.at[k, p], recv_sem=msem_r.at[k, me],
-                device_id=(mb, p), device_id_type=MESH,
-            ).start()
-
-        each_partner(body)
-        pack(make(me), mrecv.at[k, me])
+    full = cap // PACK
+    some = -(-cap // PACK)
+    height = chunks * PACK
+    cut_rows = (full * height, some * height + PACK)
+
+    def group_at(g):
+        return g * height + (PACK if g >= some else 0)
+
+    def pack(block, ref, first, count, ends_too):
+        for g in range(first, count):
+            for c in range(chunks):
+                at = group_at(g) + c * PACK
+                ref[at : at + PACK, :] = block[
+                    g * PACK : (g + 1) * PACK, c * LANE : (c + 1) * LANE
+                ].astype(bf16)
+        if ends_too:
+            ends = block[:, main:]
+            total = ends[:PACK]
+            for g in range(1, groups):
+                total = total + pltpu.roll(ends[g * PACK : (g + 1) * PACK], g * tail, 1)
+            ref[some * height : some * height + PACK, :] = total.astype(bf16)
+
+    def piece(k, p, part, slot):
+        cut_at = cut_rows[k % 2]
+        lines = pl.ds(0, cut_at) if part == 0 else pl.ds(cut_at, groups * height + PACK - cut_at)
+        return pltpu.make_async_remote_copy(
+            src_ref=msend.at[k, p, lines], dst_ref=mrecv.at[k, slot, lines],
+            send_sem=msem_s.at[k, part, p], recv_sem=msem_r.at[k, part, slot],
+            device_id=(mb, p), device_id_type=MESH,
+        )
+
+    def start(k, p, part):
+        if cut_rows[k % 2] > 0 or part == 1:
+            piece(k, p, part, me).start()
+
+    def finished(k, p, part):
+        if cut_rows[k % 2] > 0 or part == 1:
+            piece(k, p, part, p).wait()
 
     keep = iota((PACK, LANE), 1) < tail
 
-    def collect(k):
-        def unpack(p):
-            at = pl.multiple_of(p * LANE, LANE)
+    def unpack(k, p, first, count, ends_too):
+        at = pl.multiple_of(p * LANE, LANE)
+        for g in range(first, count):
             for c in range(chunks):
-                flat[pl.ds(at, slots), c * LANE : (c + 1) * LANE] = mrecv[
-                    k, p, c * slots : (c + 1) * slots, :
+                line = group_at(g) + c * PACK
+                flat[pl.ds(at + g * PACK, PACK), c * LANE : (c + 1) * LANE] = mrecv[
+                    k, p, line : line + PACK, :
                 ]
-            ends = mrecv[k, p, chunks * slots : chunks * slots + PACK, :].astype(f32)
+        if ends_too:
+            ends = mrecv[k, p, some * height : some * height + PACK, :].astype(f32)
             for g in range(groups):
                 part = ends if g == 0 else pltpu.roll(ends, LANE - g * tail, 1)
                 flat[pl.ds(at + g * PACK, PACK), main:] = jnp.where(keep, part, 0.0).astype(bf16)
 
-        unpack(me)
-
-        def body(p):
-            pltpu.make_async_remote_copy(
-                src_ref=msend.at[k, p], dst_ref=mrecv.at[k, p],
-                send_sem=msem_s.at[k, p], recv_sem=msem_r.at[k, p],
-                device_id=(mb, p), device_id_type=MESH,
-            ).wait()
-            unpack(p)
+    def half_span(first):
+        return pl.ds(pl.multiple_of(first * LANE, LANE * half), LANE * half)
+
+    def product(lhs_ref, first, count, start_at):
+        lines = half_span(start_at)
+        return dot(lhs_ref[first : first + count, lines], flat[lines, :])
+
+    def reply_all(k):
+        def body(p):
+            block = dot(pick[span(p), :], table[...])
+            pack(block, msend.at[k, p], 0, groups, True)
+            start(k, p, 0)
+            start(k, p, 1)
 
         each_partner(body)
-
-    def product(lhs_ref, first, count):
-        depth = n * LANE
-        step = min(depth, 1024)
-        total = None
-        for k in range(0, depth, step):
-            part = dot(lhs_ref[first : first + count, k : k + step], flat[k : k + step, :])
-            total = part if total is None else total + part
-        return total
+        pack(dot(pick[span(me), :], table[...]), mrecv.at[k, me], 0, groups, True)
+
+    def reply_first(k):
+        def block(p):
+            lines = pl.ds(pl.multiple_of(p * LANE, LANE), full * PACK)
+            return dot(pick[lines, :rows], table[:rows, :])
+
+        def body(p):
+            pack(block(p), msend.at[k, p], 0, full, False)
+            start(k, p, 0)
+
+        if full:
+            each_partner(body)
+            pack(block(me), mrecv.at[k, me], 0, full, False)
+
+    def reply_rest(k):
+        def body(p):
+            pack(dot(pick[span(p), :], table[...]), msend.at[k, p], full, groups, True)
+            start(k, p, 1)
+
+        each_partner(body)
+        pack(dot(pick[span(me), :], table[...]), mrecv.at[k, me], full, groups, True)
+
+    def fetch(k):
+        def body(p):
+            finished(k, p, 0)
+            finished(k, p, 1)
+            unpack(k, p, 0, groups, True)
+
+        unpack(k, me, 0, groups, True)
+        each_near(body)
+        for t in range(3):
+            fetched[t * edges : (t + 1) * edges, :] = product(place, t * edges, edges, mine)
+        each_far(body)
+        for t in range(3):
+            fetched[t * edges : (t + 1) * edges, :] += product(place, t * edges, edges, other)
+
+    def give(k):
+        def body(p):
+            block = dot(place_t[span(p), :], grads[...])
+            pack(block, msend.at[k, p], 0, groups, True)
+            start(k, p, 0)
+
+        each_partner(body)
+        each_partner(lambda p: start(k, p, 1))
+        pack(dot(place_t[span(me), :], grads[...]), mrecv.at[k, me], 0, groups, True)
+
+    def take(k, part, first):
+        lo, hi = ((0, some), (some, groups))[part]
+
+        def body(p):
+            finished(k, p, part)
+            unpack(k, p, lo, hi, part == 0)
+
+        unpack(k, me, lo, hi, part == 0)
+        each_near(body)
+        total = product(pick_t, first, rows, mine)
+        each_far(body)
+        return total + product(pick_t, first, rows, other)
 
     build_place_t(0)
     pl.semaphore_wait(barrier, n + 1)
@@ -270,7 +358,7 @@
             ask_wait(0)
             build_pick(0)
 
-        exchange(2 * s, lambda p: dot(pick[span(p), :], table[...]))
+            reply_all(0)
 
         if s == SUBS - 1:
             base_send[...] = rbuf[...].T[:width, :]
@@ -291,10 +379,7 @@
             ask_wait(1)
             build_pick(1)
 
-        collect(2 * s)
-        for t in range(3):
-            fetched[t * edges : (t + 1) * edges, :] = product(place, t * edges, edges)
-
+        fetch(2 * s)
         factor = scale[s]
         source = fetched[:edges, :] * factor
         goal = fetched[edges : 2 * edges, :]
@@ -324,11 +409,9 @@
         ).astype(bf16)
         grads[2 * edges :, :] = ((noise_grad - noise * along_n) * inv_n).astype(bf16)
 
-        exchange(2 * s + 1, lambda p: dot(place_t[span(p), :], grads[...]))
-        collect(2 * s + 1)
-
-        for buf, col, first in ((rbuf, rcol, rows), (lbuf, lcol, 0)):
-            grad = product(pick_t, first, rows)
+        give(2 * s + 1)
+        for part, (buf, col, first) in enumerate(((lbuf, lcol, 0), (rbuf, rcol, rows))):
+            grad = take(2 * s + 1, part, first)
             state = col[...][:, 0:1] + jnp.sum(grad * grad, axis=1, keepdims=True) * (1.0 / width)
             col[...] = jnp.broadcast_to(state, col.shape)
             step = rate * grad / (jnp.sqrt(state) + guard)
@@ -342,6 +425,7 @@
                 buf[...] = new
                 if s + 1 < SUBS:
                     table[first : first + rows, :] = new.astype(bf16)
+                    (reply_rest if part else reply_first)(2 * s + 2)
 
     lout_ref[...] = lbuf[...].T[:width, :]
     lsout_ref[...] = to_row(lcol[...][:, 0:1])
@@ -412,8 +496,8 @@
             pltpu.VMEM((8, rows), f32),
             pltpu.SemaphoreType.DMA((SUBS, n)),
             pltpu.SemaphoreType.DMA((SUBS, n)),
-            pltpu.SemaphoreType.DMA((2 * SUBS, n)),
-            pltpu.SemaphoreType.DMA((2 * SUBS, n)),
+            pltpu.SemaphoreType.DMA((2 * SUBS, 2, n)),
+            pltpu.SemaphoreType.DMA((2 * SUBS, 2, n)),
             pltpu.SemaphoreType.DMA((2, 3)),
             pltpu.SemaphoreType.DMA,
         ],

time: 86.4 us -> 89 us (1.030)
  the two profiles are of different devices: /device:TPU:16 before, /device:TPU:0 now
where the time goes in v2:
time: 89 us; the launch traced here: 88.9 us
  Pallas kernels  88.2 us (99%)
    pallas_call x1, Pallas kernels, on_device(): pl.pallas_call(functools.partial(kernel, n, nb, width, cap, slots), out_s...  86.2 us
    pallas_call x1, Pallas kernels, on_device(): pl.pallas_call(finish, out_shape=shapes, in_specs=[vmem] * 4, out_specs=(...  2.05 us

profile of v2, /device:TPU:0, one launch (start us, length us, event | category | flops | bytes accessed | tf_op | source)
XLA Modules:
  0.0 88.9 jit_solution(4207805645076242387)
XLA Ops:
  0.6 86.2 %shard_map.120 = (f32[400,256]{1,0:T(8,128)}, f32[1,256]{1,0:T(1,128)}, f32[400,256]{1,0:T(8,128)}, f32[1,256]{1,0:T(1,128)}) custom-call(f32[400,256]{1,0:T(8,128)} %bitcast.14, f32[400,256]{1,0:T(8,128)} %bitcast.15, f32[1,256]{1,0:T(1,128)} %bitcast.20, f32[1,256]{1,0:T(1,128)} %bitcast.21, f32[400,1024]{1,0:T(8,128)} %bitcast.13, s32[2,256]{1,0:T(2,128)} %bitcast.16, ...), custom_call_target="tpu_custom_call" | custom-call | tf_op jit(solution)/shard_map/pallas_call | solution.py:463
  86.8 2.1 %shard_map.121 = (f32[400,256]{1,0:T(8,128)}, f32[1,256]{1,0:T(1,128)}, f32[400,256]{1,0:T(8,128)}, f32[1,256]{1,0:T(1,128)}) custom-call(f32[400,256]{1,0:T(8,128)} %get-tuple-element.12.refs_0_, f32[1,256]{1,0:T(1,128)} %get-tuple-element.13.refs_1_, f32[400,256]{1,0:T(8,128)} %get-tuple-element.14.refs_2_, f32[1,256]{1,0:T(1,128)} %get-tuple-element.15.refs_3_), custom_call_target="tpu_custom_call" | custom-call | tf_op jit(solution)/shard_map/pallas_call | solution.py:511

commit v3 on v2

--- a/solution.py
+++ b/solution.py
@@ -89,8 +89,11 @@
         lax.fori_loop(1, half, step, 0)
 
     def each_partner(body):
-        each_far(body)
-        each_near(body)
+        def step(j, carry):
+            turn = n // 2 + ((j + 1) // 2) * (2 * (j % 2) - 1)
+            body(lax.rem(me + turn + n, n))
+            return carry
+        lax.fori_loop(0, n - 1, step, 0)
 
     def each_index(body):
         def step(j, carry):

time: 89 us -> 90.2 us (1.013)
  the two profiles are of different devices: /device:TPU:0 before, /device:TPU:16 now
where the time goes in v3:
time: 90.2 us; the launch traced here: 90.1 us
  Pallas kernels  89.4 us (99%)
    pallas_call x1, Pallas kernels, on_device(): pl.pallas_call(functools.partial(kernel, n, nb, width, cap, slots), out_s...  87.4 us
    pallas_call x1, Pallas kernels, on_device(): pl.pallas_call(finish, out_shape=shapes, in_specs=[vmem] * 4, out_specs=(...  2.05 us

profile of v3, /device:TPU:16, one launch (start us, length us, event | category | flops | bytes accessed | tf_op | source)
XLA Modules:
  0.0 90.1 jit_solution(16529332474919480841)
XLA Ops:
  0.6 87.4 %shard_map.120 = (f32[400,256]{1,0:T(8,128)}, f32[1,256]{1,0:T(1,128)}, f32[400,256]{1,0:T(8,128)}, f32[1,256]{1,0:T(1,128)}) custom-call(f32[400,256]{1,0:T(8,128)} %bitcast.14, f32[400,256]{1,0:T(8,128)} %bitcast.15, f32[1,256]{1,0:T(1,128)} %bitcast.20, f32[1,256]{1,0:T(1,128)} %bitcast.21, f32[400,1024]{1,0:T(8,128)} %bitcast.13, s32[2,256]{1,0:T(2,128)} %bitcast.16, ...), custom_call_target="tpu_custom_call" | custom-call | tf_op jit(solution)/shard_map/pallas_call | solution.py:466
  88.0 2.1 %shard_map.121 = (f32[400,256]{1,0:T(8,128)}, f32[1,256]{1,0:T(1,128)}, f32[400,256]{1,0:T(8,128)}, f32[1,256]{1,0:T(1,128)}) custom-call(f32[400,256]{1,0:T(8,128)} %get-tuple-element.12.refs_0_, f32[1,256]{1,0:T(1,128)} %get-tuple-element.13.refs_1_, f32[400,256]{1,0:T(8,128)} %get-tuple-element.14.refs_2_, f32[1,256]{1,0:T(1,128)} %get-tuple-element.15.refs_3_), custom_call_target="tpu_custom_call" | custom-call | tf_op jit(solution)/shard_map/pallas_call | solution.py:514

commit v4 on v1

--- a/solution.py
+++ b/solution.py
@@ -50,7 +50,7 @@
     left_ref, right_ref, lstate_ref, rstate_ref, rel_hbm, src_ref, dst_ref, kind_ref, neg_ref,
     lout_ref, lsout_ref, rout_ref, rsout_ref,
     lbuf, rbuf, lcol, rcol, table, rel_raw, rel_hi, rel_lo, scale,
-    place, place_t, pick, pick_t, prow, lrow, flat, fetched, grads,
+    place, place_t, pick, pick_t, prow, lrow, flat, fetched, grads, totals,
     wsend, wrecv, msend, mrecv, base_send, base_recv, step_send, step_recv, hist_send, hist_recv,
     wsem_s, wsem_r, msem_s, msem_r, ssem, rel_sem,
 ):
@@ -66,12 +66,32 @@
     after = lax.rem(mb + 1, nb)
     before = lax.rem(mb + nb - 1, nb)
 
-    def partner(j):
-        return lax.rem(me + n // 2 + ((j + 1) // 2) * (2 * (j % 2) - 1) + n, n)
+    half = n // 2
+    mine = (me // half) * half
+    other = half - mine
+
+    def far(j):
+        return other + lax.rem(me + j, half)
+
+    def near(j):
+        return mine + lax.rem(me + j, half)
+
+    def each_far(body):
+        def step(j, carry):
+            body(far(j))
+            return carry
+        lax.fori_loop(0, half, step, 0)
+
+    def each_near(body):
+        def step(j, carry):
+            body(near(j))
+            return carry
+        lax.fori_loop(1, half, step, 0)
 
     def each_partner(body):
         def step(j, carry):
-            body(partner(j))
+            turn = n // 2 + ((j + 1) // 2) * (2 * (j % 2) - 1)
+            body(lax.rem(me + turn + n, n))
             return carry
         lax.fori_loop(0, n - 1, step, 0)
 
@@ -104,7 +124,8 @@
 
     earlier = one_hot(iota((edges, edges), 0) < iota((edges, edges), 1))
     holder = iota((n, edges), 0)
-    for s in range(SUBS):
+
+    def find(s):
         for t, ids_ref in enumerate((src_ref, dst_ref, neg_ref)):
             ids = ids_ref[s : s + 1, :]
             inside = (ids >= holder * rows) & (ids < holder * rows + rows)
@@ -136,24 +157,22 @@
 
             each_index(body)
 
-    def ask(s):
+    def prepare(s):
         local = lrow[s : s + 1, :]
         upper = iota((8, 3 * edges), 0)
         lhs = jnp.where(upper == 0, local, jnp.where(upper == 1, 1.0, 0.0)).astype(bf16)
         lane = iota((1, LANE), 1)
         offset = jnp.where(lane < cap, 0.0, float(rows))
 
-        def wanted(p):
-            found = dot(lhs, place_t[span(p), :], ((1,), (1,)))
-            row = jnp.where(found[1:2] > 0.5, found[0:1] + offset, -1.0)
-            return jnp.broadcast_to(row, (8, LANE))
-
-        def body(p):
-            wsend[s, p] = wanted(p)
-            ask_copy(s, p).start()
-
-        each_partner(body)
-        wrecv[s, me] = wanted(me)
+        found = dot(lhs, place_t[...], ((1,), (1,)))
+        for p in range(n):
+            part = found[:, p * LANE : (p + 1) * LANE]
+            row = jnp.where(part[1:2] > 0.5, part[0:1] + offset, -1.0)
+            wsend[s, p] = jnp.broadcast_to(row, (8, LANE))
+
+    def ask(s):
+        each_partner(lambda p: ask_copy(s, p).start())
+        wrecv[s, me] = wsend[s, me]
 
     def ask_copy(s, p):
         return pltpu.make_async_remote_copy(
@@ -173,12 +192,9 @@
 
         each_partner(body)
 
-    def build_pick(s):
-        def body(p):
-            column = to_column(wrecv[s, p][0:1, :]).astype(jnp.int32)
-            pick[span(p), :] = one_hot(iota((LANE, 2 * rows), 1) == column)
-
-        each_index(body)
+    def build_pick(s, p):
+        column = to_column(wrecv[s, p][0:1, :]).astype(jnp.int32)
+        pick[span(p), :] = one_hot(iota((LANE, 2 * rows), 1) == column)
 
     def build_pick_t(s):
         def body(p):
@@ -196,66 +212,74 @@
             total = total + pltpu.roll(ends[g * PACK : (g + 1) * PACK], g * tail, 1)
         ref[chunks * slots :, :] = total.astype(bf16)
 
+    def piece(k, p, slot):
+        return pltpu.make_async_remote_copy(
+            src_ref=msend.at[k, p], dst_ref=mrecv.at[k, slot],
+            send_sem=msem_s.at[k, p], recv_sem=msem_r.at[k, slot],
+            device_id=(mb, p), device_id_type=MESH,
+        )
+
+    keep = iota((PACK, LANE), 1) < tail
+
+    def unpack(k, p):
+        at = pl.multiple_of(p * LANE, LANE)
+        for c in range(chunks):
+            flat[pl.ds(at, slots), c * LANE : (c + 1) * LANE] = mrecv[
+                k, p, c * slots : (c + 1) * slots, :
+            ]
+        ends = mrecv[k, p, chunks * slots : chunks * slots + PACK, :].astype(f32)
+        for g in range(groups):
+            part = ends if g == 0 else pltpu.roll(ends, LANE - g * tail, 1)
+            flat[pl.ds(at + g * PACK, PACK), main:] = jnp.where(keep, part, 0.0).astype(bf16)
+
+    def arrive(k):
+        def body(p):
+            piece(k, p, p).wait()
+            unpack(k, p)
+
+        return body
+
     def exchange(k, make):
         def body(p):
             pack(make(p), msend.at[k, p])
-            pltpu.make_async_remote_copy(
-                src_ref=msend.at[k, p], dst_ref=mrecv.at[k, me],
-                send_sem=msem_s.at[k, p], recv_sem=msem_r.at[k, me],
-                device_id=(mb, p), device_id_type=MESH,
-            ).start()
+            piece(k, p, me).start()
 
         each_partner(body)
         pack(make(me), mrecv.at[k, me])
 
-    keep = iota((PACK, LANE), 1) < tail
-
-    def collect(k):
-        def unpack(p):
-            at = pl.multiple_of(p * LANE, LANE)
-            for c in range(chunks):
-                flat[pl.ds(at, slots), c * LANE : (c + 1) * LANE] = mrecv[
-                    k, p, c * slots : (c + 1) * slots, :
-                ]
-            ends = mrecv[k, p, chunks * slots : chunks * slots + PACK, :].astype(f32)
-            for g in range(groups):
-                part = ends if g == 0 else pltpu.roll(ends, LANE - g * tail, 1)
-                flat[pl.ds(at + g * PACK, PACK), main:] = jnp.where(keep, part, 0.0).astype(bf16)
-
-        unpack(me)
-
-        def body(p):
-            pltpu.make_async_remote_copy(
-                src_ref=msend.at[k, p], dst_ref=mrecv.at[k, p],
-                send_sem=msem_s.at[k, p], recv_sem=msem_r.at[k, p],
-                device_id=(mb, p), device_id_type=MESH,
-            ).wait()
-            unpack(p)
-
-        each_partner(body)
-
-    def product(lhs_ref, first, count):
-        depth = n * LANE
-        step = min(depth, 1024)
-        total = None
-        for k in range(0, depth, step):
-            part = dot(lhs_ref[first : first + count, k : k + step], flat[k : k + step, :])
-            total = part if total is None else total + part
-        return total
-
+    def half_span(first):
+        return pl.ds(pl.multiple_of(first * LANE, LANE * half), LANE * half)
+
+    def product(lhs_ref, first, count, start_at):
+        lines = half_span(start_at)
+        return dot(lhs_ref[first : first + count, lines], flat[lines, :])
+
+    def fetch(k):
+        unpack(k, me)
+        each_near(arrive(k))
+        for t in range(3):
+            fetched[t * edges : (t + 1) * edges, :] = product(place, t * edges, edges, mine)
+        each_far(arrive(k))
+        for t in range(3):
+            fetched[t * edges : (t + 1) * edges, :] += product(place, t * edges, edges, other)
+
+    def take(k):
+        unpack(k, me)
+        each_near(arrive(k))
+        for first in (rows, 0):
+            totals[first : first + rows, :] = product(pick_t, first, rows, mine)
+        each_far(arrive(k))
+
+    find(0)
     build_place_t(0)
+    prepare(0)
     pl.semaphore_wait(barrier, n + 1)
     ask(0)
 
-    for buf, ref in ((lbuf, left_ref), (rbuf, right_ref)):
-        buf[...] = jnp.concatenate([ref[...], jnp.zeros((wide - width, rows), f32)], axis=0).T
-    lcol[...] = jnp.broadcast_to(to_column(lstate_ref[...]), lcol.shape)
-    rcol[...] = jnp.broadcast_to(to_column(rstate_ref[...]), rcol.shape)
-    table[:rows, :] = lbuf[...].astype(bf16)
-    table[rows:, :] = rbuf[...].astype(bf16)
-    flat[...] = jnp.zeros(flat.shape, bf16)
-    build_place_t(1)
-    ask(1)
+    for buf, ref, first in ((lbuf, left_ref, 0), (rbuf, right_ref, rows)):
+        turned = jnp.concatenate([ref[...], jnp.zeros((wide - width, rows), f32)], axis=0).T
+        buf[...] = turned
+        table[first : first + rows, :] = turned.astype(bf16)
 
     rel_count = rel_raw.shape[1]
 
@@ -266,15 +290,26 @@
         scale[s] = dot(chosen, rel_hi[...], last) + dot(chosen, rel_lo[...], last)
 
     for s in range(SUBS):
+        def reply(p):
+            if s == 0:
+                build_pick(0, p)
+            return dot(pick[span(p), :], table[...])
+
         if s == 0:
             ask_wait(0)
-            build_pick(0)
-
-        exchange(2 * s, lambda p: dot(pick[span(p), :], table[...]))
+        exchange(2 * s, reply)
 
         if s == SUBS - 1:
             base_send[...] = rbuf[...].T[:width, :]
             onward(base_send, base_recv, 0).start()
+        if s == 0:
+            find(1)
+            build_place_t(1)
+            prepare(1)
+            ask(1)
+            lcol[...] = jnp.broadcast_to(to_column(lstate_ref[...]), lcol.shape)
+            rcol[...] = jnp.broadcast_to(to_column(rstate_ref[...]), rcol.shape)
+            flat[...] = jnp.zeros(flat.shape, bf16)
         build_place(s)
         build_place_t(s)
         build_pick_t(s)
@@ -289,12 +324,9 @@
             set_scale(0)
             set_scale(1)
             ask_wait(1)
-            build_pick(1)
-
-        collect(2 * s)
-        for t in range(3):
-            fetched[t * edges : (t + 1) * edges, :] = product(place, t * edges, edges)
-
+            each_index(lambda p: build_pick(1, p))
+
+        fetch(2 * s)
         factor = scale[s]
         source = fetched[:edges, :] * factor
         goal = fetched[edges : 2 * edges, :]
@@ -325,10 +357,9 @@
         grads[2 * edges :, :] = ((noise_grad - noise * along_n) * inv_n).astype(bf16)
 
         exchange(2 * s + 1, lambda p: dot(place_t[span(p), :], grads[...]))
-        collect(2 * s + 1)
-
+        take(2 * s + 1)
         for buf, col, first in ((rbuf, rcol, rows), (lbuf, lcol, 0)):
-            grad = product(pick_t, first, rows)
+            grad = totals[first : first + rows, :] + product(pick_t, first, rows, other)
             state = col[...][:, 0:1] + jnp.sum(grad * grad, axis=1, keepdims=True) * (1.0 / width)
             col[...] = jnp.broadcast_to(state, col.shape)
             step = rate * grad / (jnp.sqrt(state) + guard)
@@ -400,6 +431,7 @@
             pltpu.VMEM((n * LANE, wide), bf16),
             pltpu.VMEM((3 * edges, wide), f32),
             pltpu.VMEM((3 * edges, wide), bf16),
+            pltpu.VMEM((2 * rows, wide), f32),
             pltpu.VMEM((SUBS, n, 8, LANE), f32),
             pltpu.VMEM((SUBS, n, 8, LANE), f32),
             pltpu.VMEM((2 * SUBS, n, message, LANE), bf16),

time: 86.4 us -> 91.5 us (1.059); the launches traced: 84.9 us -> 91.3 us
  Pallas kernels: 84.3 us -> 90.7 us
    pallas_call x1, Pallas kernels: 82.2 us -> 88.6 us  [on_device(): pl.pallas_call(functools.partial(kernel, n, nb, width, cap, slots), out_s...]
where the time goes in v4:
time: 91.5 us; the launch traced here: 91.3 us
  Pallas kernels  90.7 us (99%)
    pallas_call x1, Pallas kernels, on_device(): pl.pallas_call(functools.partial(kernel, n, nb, width, cap, slots), out_s...  88.6 us
    pallas_call x1, Pallas kernels, on_device(): pl.pallas_call(finish, out_shape=shapes, in_specs=[vmem] * 4, out_specs=(...  2.05 us

profile of v4, /device:TPU:16, one launch (start us, length us, event | category | flops | bytes accessed | tf_op | source)
XLA Modules:
  0.0 91.3 jit_solution(1524706211386106281)
XLA Ops:
  0.6 88.6 %shard_map.120 = (f32[400,256]{1,0:T(8,128)}, f32[1,256]{1,0:T(1,128)}, f32[400,256]{1,0:T(8,128)}, f32[1,256]{1,0:T(1,128)}) custom-call(f32[400,256]{1,0:T(8,128)} %bitcast.14, f32[400,256]{1,0:T(8,128)} %bitcast.15, f32[1,256]{1,0:T(1,128)} %bitcast.20, f32[1,256]{1,0:T(1,128)} %bitcast.21, f32[400,1024]{1,0:T(8,128)} %bitcast.13, s32[2,256]{1,0:T(2,128)} %bitcast.16, ...), custom_call_target="tpu_custom_call" | custom-call | tf_op jit(solution)/shard_map/pallas_call | solution.py:410
  89.3 2.1 %shard_map.121 = (f32[400,256]{1,0:T(8,128)}, f32[1,256]{1,0:T(1,128)}, f32[400,256]{1,0:T(8,128)}, f32[1,256]{1,0:T(1,128)}) custom-call(f32[400,256]{1,0:T(8,128)} %get-tuple-element.12.refs_0_, f32[1,256]{1,0:T(1,128)} %get-tuple-element.13.refs_1_, f32[400,256]{1,0:T(8,128)} %get-tuple-element.14.refs_2_, f32[1,256]{1,0:T(1,128)} %get-tuple-element.15.refs_3_), custom_call_target="tpu_custom_call" | custom-call | tf_op jit(solution)/shard_map/pallas_call | solution.py:459

commit v5 on v4

--- a/solution.py
+++ b/solution.py
@@ -50,7 +50,7 @@
     left_ref, right_ref, lstate_ref, rstate_ref, rel_hbm, src_ref, dst_ref, kind_ref, neg_ref,
     lout_ref, lsout_ref, rout_ref, rsout_ref,
     lbuf, rbuf, lcol, rcol, table, rel_raw, rel_hi, rel_lo, scale,
-    place, place_t, pick, pick_t, prow, lrow, flat, fetched, grads, totals,
+    place, place_t, pick, pick_t, prow, lrow, flat, fetched, grads,
     wsend, wrecv, msend, mrecv, base_send, base_recv, step_send, step_recv, hist_send, hist_recv,
     wsem_s, wsem_r, msem_s, msem_r, ssem, rel_sem,
 ):
@@ -66,28 +66,6 @@
     after = lax.rem(mb + 1, nb)
     before = lax.rem(mb + nb - 1, nb)
 
-    half = n // 2
-    mine = (me // half) * half
-    other = half - mine
-
-    def far(j):
-        return other + lax.rem(me + j, half)
-
-    def near(j):
-        return mine + lax.rem(me + j, half)
-
-    def each_far(body):
-        def step(j, carry):
-            body(far(j))
-            return carry
-        lax.fori_loop(0, half, step, 0)
-
-    def each_near(body):
-        def step(j, carry):
-            body(near(j))
-            return carry
-        lax.fori_loop(1, half, step, 0)
-
     def each_partner(body):
         def step(j, carry):
             turn = n // 2 + ((j + 1) // 2) * (2 * (j % 2) - 1)
@@ -99,7 +77,7 @@
         def step(j, carry):
             body(j)
             return carry
-        lax.fori_loop(0, n, step, 0)
+        lax.fori_loop(0, n, step, 0, unroll=n <= 8)
 
     barrier = pltpu.get_barrier_semaphore()
 
@@ -142,7 +120,7 @@
         row = prow[s : s + 1, :].astype(jnp.int32)
 
         def body(p):
-            place_t[span(p), :] = one_hot(iota((LANE, 3 * edges), 0) + p * LANE == row)
+            place_t[s, span(p), :] = one_hot(iota((LANE, 3 * edges), 0) + p * LANE == row)
 
         each_index(body)
 
@@ -164,7 +142,7 @@
         lane = iota((1, LANE), 1)
         offset = jnp.where(lane < cap, 0.0, float(rows))
 
-        found = dot(lhs, place_t[...], ((1,), (1,)))
+        found = dot(lhs, place_t[s], ((1,), (1,)))
         for p in range(n):
             part = found[:, p * LANE : (p + 1) * LANE]
             row = jnp.where(part[1:2] > 0.5, part[0:1] + offset, -1.0)
@@ -247,28 +225,18 @@
         each_partner(body)
         pack(make(me), mrecv.at[k, me])
 
-    def half_span(first):
-        return pl.ds(pl.multiple_of(first * LANE, LANE * half), LANE * half)
-
-    def product(lhs_ref, first, count, start_at):
-        lines = half_span(start_at)
-        return dot(lhs_ref[first : first + count, lines], flat[lines, :])
-
-    def fetch(k):
+    def product(lhs_ref, first, count):
+        depth = n * LANE
+        step = min(depth, 1024)
+        total = None
+        for k in range(0, depth, step):
+            part = dot(lhs_ref[first : first + count, k : k + step], flat[k : k + step, :])
+            total = part if total is None else total + part
+        return total
+
+    def collect(k):
         unpack(k, me)
-        each_near(arrive(k))
-        for t in range(3):
-            fetched[t * edges : (t + 1) * edges, :] = product(place, t * edges, edges, mine)
-        each_far(arrive(k))
-        for t in range(3):
-            fetched[t * edges : (t + 1) * edges, :] += product(place, t * edges, edges, other)
-
-    def take(k):
-        unpack(k, me)
-        each_near(arrive(k))
-        for first in (rows, 0):
-            totals[first : first + rows, :] = product(pick_t, first, rows, mine)
-        each_far(arrive(k))
+        each_partner(arrive(k))
 
     find(0)
     build_place_t(0)
@@ -310,8 +278,8 @@
             lcol[...] = jnp.broadcast_to(to_column(lstate_ref[...]), lcol.shape)
             rcol[...] = jnp.broadcast_to(to_column(rstate_ref[...]), rcol.shape)
             flat[...] = jnp.zeros(flat.shape, bf16)
-        build_place(s)
-        build_place_t(s)
+        if s == 0:
+            build_place(0)
         build_pick_t(s)
         if s == 0:
             rel_copy.wait()
@@ -322,11 +290,11 @@
             rel_hi[:width, :] = upper
             rel_lo[:width, :] = (raw - upper.astype(f32)).astype(bf16)
             set_scale(0)
-            set_scale(1)
-            ask_wait(1)
-            each_index(lambda p: build_pick(1, p))
-
-        fetch(2 * s)
+
+        collect(2 * s)
+        for t in range(3):
+            fetched[t * edges : (t + 1) * edges, :] = product(place, t * edges, edges)
+
         factor = scale[s]
         source = fetched[:edges, :] * factor
         goal = fetched[edges : 2 * edges, :]
@@ -356,10 +324,15 @@
         ).astype(bf16)
         grads[2 * edges :, :] = ((noise_grad - noise * along_n) * inv_n).astype(bf16)
 
-        exchange(2 * s + 1, lambda p: dot(place_t[span(p), :], grads[...]))
-        take(2 * s + 1)
+        exchange(2 * s + 1, lambda p: dot(place_t[s, span(p), :], grads[...]))
+        if s + 1 < SUBS:
+            ask_wait(s + 1)
+            each_index(lambda p: build_pick(s + 1, p))
+            build_place(s + 1)
+            set_scale(s + 1)
+        collect(2 * s + 1)
         for buf, col, first in ((rbuf, rcol, rows), (lbuf, lcol, 0)):
-            grad = totals[first : first + rows, :] + product(pick_t, first, rows, other)
+            grad = product(pick_t, first, rows)
             state = col[...][:, 0:1] + jnp.sum(grad * grad, axis=1, keepdims=True) * (1.0 / width)
             col[...] = jnp.broadcast_to(state, col.shape)
             step = rate * grad / (jnp.sqrt(state) + guard)
@@ -423,7 +396,7 @@
             pltpu.VMEM((wide, rel_count), bf16),
             pltpu.VMEM((SUBS, edges, wide), f32),
             pltpu.VMEM((3 * edges, n * LANE), bf16),
-            pltpu.VMEM((n * LANE, 3 * edges), bf16),
+            pltpu.VMEM((SUBS, n * LANE, 3 * edges), bf16),
             pltpu.VMEM((n * LANE, 2 * rows), bf16),
             pltpu.VMEM((2 * rows, n * LANE), bf16),
             pltpu.VMEM((8, 3 * edges), f32),
@@ -431,7 +404,6 @@
             pltpu.VMEM((n * LANE, wide), bf16),
             pltpu.VMEM((3 * edges, wide), f32),
             pltpu.VMEM((3 * edges, wide), bf16),
-            pltpu.VMEM((2 * rows, wide), f32),
             pltpu.VMEM((SUBS, n, 8, LANE), f32),
             pltpu.VMEM((SUBS, n, 8, LANE), f32),
             pltpu.VMEM((2 * SUBS, n, message, LANE), bf16),

time: 91.5 us -> 88.8 us (0.970)
  Pallas kernels: 90.7 us -> 88 us
    pallas_call x1, Pallas kernels: 88.6 us -> 85.9 us  [on_device(): pl.pallas_call(functools.partial(kernel, n, nb, width, cap, slots), out_s...]
where the time goes in v5:
time: 88.8 us; the launch traced here: 88.6 us
  Pallas kernels  88 us (99%)
    pallas_call x1, Pallas kernels, on_device(): pl.pallas_call(functools.partial(kernel, n, nb, width, cap, slots), out_s...  85.9 us
    pallas_call x1, Pallas kernels, on_device(): pl.pallas_call(finish, out_shape=shapes, in_specs=[vmem] * 4, out_specs=(...  2.05 us

profile of v5, /device:TPU:16, one launch (start us, length us, event | category | flops | bytes accessed | tf_op | source)
XLA Modules:
  0.0 88.6 jit_solution(3262240707202510032)
XLA Ops:
  0.6 85.9 %shard_map.120 = (f32[400,256]{1,0:T(8,128)}, f32[1,256]{1,0:T(1,128)}, f32[400,256]{1,0:T(8,128)}, f32[1,256]{1,0:T(1,128)}) custom-call(f32[400,256]{1,0:T(8,128)} %bitcast.14, f32[400,256]{1,0:T(8,128)} %bitcast.15, f32[1,256]{1,0:T(1,128)} %bitcast.20, f32[1,256]{1,0:T(1,128)} %bitcast.21, f32[400,1024]{1,0:T(8,128)} %bitcast.13, s32[2,256]{1,0:T(2,128)} %bitcast.16, ...), custom_call_target="tpu_custom_call" | custom-call | tf_op jit(solution)/shard_map/pallas_call | solution.py:383
  86.5 2.1 %shard_map.121 = (f32[400,256]{1,0:T(8,128)}, f32[1,256]{1,0:T(1,128)}, f32[400,256]{1,0:T(8,128)}, f32[1,256]{1,0:T(1,128)}) custom-call(f32[400,256]{1,0:T(8,128)} %get-tuple-element.12.refs_0_, f32[1,256]{1,0:T(1,128)} %get-tuple-element.13.refs_1_, f32[400,256]{1,0:T(8,128)} %get-tuple-element.14.refs_2_, f32[1,256]{1,0:T(1,128)} %get-tuple-element.15.refs_3_), custom_call_target="tpu_custom_call" | custom-call | tf_op jit(solution)/shard_map/pallas_call | solution.py:431
